TPU v7x, 256 devices: a whole 4x4x8 slice. The times are simulated.
256 devices in a mesh: dp: 4 (over y_lo, core), row: 8 (over x, y_hi), col: 8 (over z).
Axes of the slice: x: 4, y: 4 (y_hi: 2, y_lo: 2; y = y_hi * 2 + y_lo), z: 8, core: 2. Of those that a mesh axis runs over, the one named last changes fastest.
Arguments:
- inputs: bfloat16 [2048, 6144], P('dp', 'row'), may hold values from -600 to 600
- saved_qkv: bfloat16 [2048, 3, 3072], P('dp', None, 'col'), may hold values from -6 to 6
- saved_up: bfloat16 [2048, 12288], P('dp', 'col'), may hold values from -6 to 6
- cotangent: bfloat16 [2048, 6144], P('dp', 'row'), may hold values from -6 to 6
- weight_qkv: bfloat16 [6144, 3, 3072], P('row', None, 'col'), may hold values from -0.078125 to 0.078125
- weight_up: bfloat16 [6144, 12288], P('row', 'col'), may hold values from -0.078125 to 0.078125
- weight_attn: bfloat16 [3072, 6144], P('col', 'row'), may hold values from -0.109375 to 0.109375
- weight_down: bfloat16 [12288, 6144], P('col', 'row'), may hold values from -0.0546875 to 0.0546875
Outputs:
- grad_inputs: bfloat16 [2048, 6144], P(('dp', 'col'), 'row')
- grad_qkv: bfloat16 [8, 4, 192, 3, 3072], P('row', 'dp', None, None, 'col')
- grad_up: bfloat16 [8, 4, 192, 12288], P('row', 'dp', None, 'col')
- grad_attn: bfloat16 [8, 4, 96, 6144], P('col', 'dp', None, 'row')
- grad_down: bfloat16 [8, 4, 384, 6144], P('col', 'dp', None, 'row')
All inputs are finite; a program needn't handle non-finite values.
Results may differ from a plain program's by a relative error of at most 0.0039.
The roundings to bfloat16 on the way count: a program that leaves them out, or rounds other values in their place, can miss the bound.
Values may be sent and summed in bfloat16 or wider, within the bound.
A program may use at most 128 MiB of HBM per device.

v0:
```python
import jax
import jax.numpy as jnp
from jax import lax
from jax.sharding import PartitionSpec as P

HD = 128
S = 256


EPS = 1e-06
SQRT_HALF = 0.7071067811865476
INV_ROOT_TWO_PI = 0.3989422804014327


def gelu_exact(values):
    return 0.5 * values * (1.0 + jax.scipy.special.erf(values * SQRT_HALF))


def gelu_slope(values):
    cumul = 0.5 * (1.0 + jax.scipy.special.erf(values * SQRT_HALF))
    return cumul + values * jnp.exp(-0.5 * values * values) * INV_ROOT_TWO_PI


def head_norm(values):
    average = jnp.mean(values, axis=-1, keepdims=True)
    centred = values - average
    inv_std = lax.rsqrt(jnp.mean(centred * centred, axis=-1, keepdims=True) + EPS)
    return (centred * inv_std, inv_std)


def head_norm_back(normed, inv_std, upstream):
    first = jnp.mean(upstream, axis=-1, keepdims=True)
    cross = jnp.mean(upstream * normed, axis=-1, keepdims=True)
    return inv_std * (upstream - first - normed * cross)


def body(inputs, saved_qkv, saved_up, cotangent, weight_qkv, weight_up, weight_attn, weight_down):
    f32 = jnp.float32
    bf16 = jnp.bfloat16
    tok_rows, feat_local = inputs.shape
    head_cols = saved_qkv.shape[2]
    up_cols = saved_up.shape[1]
    n_row = lax.axis_size("row")
    n_col = lax.axis_size("col")
    width = feat_local * n_row
    head_count = head_cols // HD
    images = tok_rows // S
    values = inputs.astype(f32)
    first_sum, square_sum = lax.psum(
        (jnp.sum(values, axis=1), jnp.sum(values * values, axis=1)), "row"
    )
    average = (first_sum / width)[:, None]
    inv_std = lax.rsqrt((square_sum / width)[:, None] - average * average + EPS)
    normed = (values - average) * inv_std
    normed_b = normed.astype(bf16)
    qkv5 = saved_qkv.reshape(images, S, 3, head_count, HD)
    query = qkv5[:, :, 0]
    keyed = qkv5[:, :, 1]
    valued = qkv5[:, :, 2]
    q_norm, q_inv = head_norm(query.astype(f32))
    k_norm, k_inv = head_norm(keyed.astype(f32))
    qn_b = q_norm.astype(bf16)
    kn_b = k_norm.astype(bf16)
    scale = HD ** (-0.5)
    scores = jnp.einsum("bqhd,bkhd->bhqk", qn_b, kn_b, preferred_element_type=f32) * scale
    expo = jnp.exp(scores)
    probs = expo / jnp.sum(expo, axis=-1, keepdims=True)
    probs_b = probs.astype(bf16)
    attended = jnp.einsum("bhqk,bkhd->bqhd", probs_b, valued, preferred_element_type=f32).astype(
        bf16
    )
    attended = attended.reshape(tok_rows, head_cols)
    hidden_b = gelu_exact(saved_up.astype(f32)).astype(bf16)
    part_attn = jnp.einsum("td,ad->ta", cotangent, weight_attn, preferred_element_type=f32)
    part_hidden = jnp.einsum("td,fd->tf", cotangent, weight_down, preferred_element_type=f32)
    sum_attn, sum_hidden = lax.psum((part_attn, part_hidden), "row")
    grad_o = sum_attn.astype(bf16)
    grad_pre = (sum_hidden * gelu_slope(saved_up.astype(f32))).astype(bf16)
    grad_o4 = grad_o.reshape(images, S, head_count, HD)
    grad_probs = jnp.einsum("bqhd,bkhd->bhqk", grad_o4, valued, preferred_element_type=f32)
    grad_value = jnp.einsum("bhqk,bqhd->bkhd", probs_b, grad_o4, preferred_element_type=f32).astype(
        bf16
    )
    rowdot = jnp.sum(probs * grad_probs, axis=-1, keepdims=True)
    grad_scores = (probs * (grad_probs - rowdot) * scale).astype(bf16)
    grad_qn = jnp.einsum("bhqk,bkhd->bqhd", grad_scores, kn_b, preferred_element_type=f32)
    grad_kn = jnp.einsum("bhqk,bqhd->bkhd", grad_scores, qn_b, preferred_element_type=f32)
    grad_query = head_norm_back(q_norm, q_inv, grad_qn).astype(bf16)
    grad_key = head_norm_back(k_norm, k_inv, grad_kn).astype(bf16)
    grad_flat = jnp.stack([grad_query, grad_key, grad_value], axis=2).reshape(
        tok_rows, 3 * head_cols
    )
    flat_weight = weight_qkv.reshape(feat_local, 3 * head_cols)
    share_rows = tok_rows // n_col
    total = jnp.einsum("ta,da->td", grad_flat, flat_weight, preferred_element_type=f32)
    grad_normed = lax.psum_scatter(
        total + jnp.einsum("tf,df->td", grad_pre, weight_up, preferred_element_type=f32),
        "col",
        scatter_dimension=0,
        tiled=True,
    )
    first_row = lax.axis_index("col") * share_rows
    normed_share = lax.dynamic_slice_in_dim(normed, first_row, share_rows, 0)
    inv_share = lax.dynamic_slice_in_dim(inv_std, first_row, share_rows, 0)
    cot_share = lax.dynamic_slice_in_dim(cotangent, first_row, share_rows, 0)
    sum_grad, sum_cross = lax.psum(
        (jnp.sum(grad_normed, axis=1), jnp.sum(grad_normed * normed_share, axis=1)), "row"
    )
    branch_term = (
        grad_normed - (sum_grad / width)[:, None] - normed_share * (sum_cross / width)[:, None]
    )
    grad_inputs = (cot_share.astype(f32) + inv_share * branch_term).astype(bf16)
    part_qkv = jnp.einsum("td,ta->da", normed_b, grad_flat, preferred_element_type=f32)
    part_up = jnp.einsum("td,tf->df", normed_b, grad_pre, preferred_element_type=f32)
    part_weight_attn = jnp.einsum("ta,td->ad", attended, cotangent, preferred_element_type=f32)
    part_down = jnp.einsum("tf,td->fd", hidden_b, cotangent, preferred_element_type=f32)
    summed_qkv, summed_up, summed_attn, summed_down = (
        lax.psum_scatter(part_qkv, "dp", scatter_dimension=0, tiled=True),
        lax.psum_scatter(part_up, "dp", scatter_dimension=0, tiled=True),
        lax.psum_scatter(part_weight_attn, "dp", scatter_dimension=0, tiled=True),
        lax.psum_scatter(part_down, "dp", scatter_dimension=0, tiled=True),
    )
    grad_qkv = summed_qkv.astype(bf16).reshape(1, 1, summed_qkv.shape[0], 3, head_cols)
    grad_up = summed_up.astype(bf16).reshape(1, 1, summed_up.shape[0], up_cols)
    grad_attn = summed_attn.astype(bf16).reshape(1, 1, summed_attn.shape[0], feat_local)
    grad_down = summed_down.astype(bf16).reshape(1, 1, summed_down.shape[0], feat_local)
    return (grad_inputs, grad_qkv, grad_up, grad_attn, grad_down)


def solution(mesh):
    return jax.shard_map(
        body,
        mesh=mesh,
        in_specs=(
            P("dp", "row"),
            P("dp", None, "col"),
            P("dp", "col"),
            P("dp", "row"),
            P("row", None, "col"),
            P("row", "col"),
            P("col", "row"),
            P("col", "row"),
        ),
        out_specs=(
            P(("dp", "col"), "row"),
            P("row", "dp", None, None, "col"),
            P("row", "dp", None, "col"),
            P("col", "dp", None, "row"),
            P("col", "dp", None, "row"),
        ),
        check_vma=False,
    )
```

profile of v0, /device:TPU:24, one launch (start us, length us, event | category | flops | bytes accessed | tf_op | source)
XLA Modules:
  0.0 420.2 jit_solution(3043145020567585647)
XLA Ops:
  8.1 1.6 copy-done
  9.7 4.3 %fusion.98 = f32[512,1536]{1,0:T(8,128)} fusion(bf16[512,768]{1,0:T(8,128)(2,1)} %param.11, bf16[1536,768]{1,0:T(8,128)(2,1)S(1)} %copy-done), kind=kOutput, calls=%fused_computation.108 | convolution fusion | flops 1207959552 | bytes 6291456 | tf_op jit(solution)/shard_map/td,fd->tf/dot_general | solution.py:75
  14.0 1.6 copy.25
  15.6 1.2 reshape.91
  16.8 2.9 fusion.88
  19.7 1.3 copy.50
  21.3 0.6 add_rsqrt_fusion
  22.0 0.6 add_rsqrt_fusion.1
  22.6 2.5 fusion.55
  25.0 2.6 fusion.31
  27.6 1.5 copy.40
  29.2 2.6 fusion.100
  31.9 2.9 fusion.97
  34.9 0.9 convert_reduce_fusion
  35.8 74.5 %all-reduce.6 = (bf16[512,384]{1,0:T(8,128)(2,1)S(1)}, f32[512]{0:T(512)}, f32[512]{0:T(512)}) all-reduce(f32[512,384]{1,0:T(8,128)} %fusion.97, f32[512]{0:T(512)} %get-tuple-element.16, f32[512]{0:T(512)} %get-tuple-element.15), channel_id=1, replica_groups=mesh['dp'=4,'row'=8,'col'=8] {'row'}, use_global_device_ids=true, to_apply=%region_9.0 | all-reduce | flops 197632 | bytes 1187840 | tf_op jit(solution)/shard_map/psum | solution.py:76
  110.2 0.9 reshape.100
  111.1 1.2 copy.35
  112.4 2.6 fusion.61
  115.0 5.1 %fusion.86 = (f32[2,256,3]{1,2,0:T(4,128)}, f32[2,256,3]{1,2,0:T(4,128)}, f32[2,256,3,128]{1,3,2,0:T(8,128)}) fusion(f32[2,256,3]{1,2,0:T(4,128)} %add_rsqrt_fusion, f32[2,256,3]{1,2,0:T(4,128)S(1)} %broadcast_multiply_fusion.4, bf16[2,256,1,3,128]{1,0,4,3,2:T(2,128)(2,1)S(1)} %get-tuple-element.30, f32[2,3,256,256]{2,3,1,0:T(8,128)} %fusion.55, ...), kind=kOutput, calls=%fused_computation.104 | convolution fusion | flops 104594176 | bytes 4755456 | tf_op jit(solution)/shard_map/bhqk,bqhd->bkhd/dot_general | solution.py:87
  120.1 5.1 %fusion.85 = (f32[2,256,3]{1,2,0:T(4,128)}, f32[2,256,3]{1,2,0:T(4,128)}, f32[2,256,3,128]{1,3,2,0:T(8,128)}) fusion(f32[2,256,3]{1,2,0:T(4,128)} %add_rsqrt_fusion.1, f32[2,256,3]{1,2,0:T(4,128)S(1)} %broadcast_multiply_fusion.5, bf16[2,256,1,3,128]{1,0,4,3,2:T(2,128)(2,1)S(1)} %get-tuple-element.29, f32[2,3,256,256]{2,3,1,0:T(8,128)} %fusion.55, ...), kind=kOutput, calls=%fused_computation.103 | convolution fusion | flops 104594176 | bytes 4755456 | tf_op jit(solution)/shard_map/bhqk,bkhd->bqhd/dot_general | solution.py:86
  125.2 0.8 broadcast_multiply_fusion
  126.0 0.7 broadcast_multiply_fusion.1
  126.7 0.7 broadcast_multiply_fusion.2
  127.4 0.7 broadcast_multiply_fusion.3
  128.1 1.9 fusion.30
  130.6 1.2 copy.37
  132.1 4.3 %copy.38 = bf16[768,3,384]{0,2,1:T(8,128)(2,1)} copy(bf16[768,3,384]{2,0,1:T(8,128)(2,1)} %param.12) | data formatting | bytes 3538944 | tf_op args[4]
  136.3 70.1 %all-reduce.5.cloned.1.call-done = f32[512,1536]{1,0:T(8,128)} async-done(((f32[512,1536]{1,0:T(8,128)}), f32[512,1536]{1,0:T(8,128)}) %all-reduce.5.cloned.1.call-update) | async-done | bytes 3145744 | tf_op jit(solution)/shard_map/psum | solution.py:76
  206.4 3.2 fusion.7
  209.6 1.4 fusion.99
  211.6 2.4 convolution_add_fusion
  215.2 4.5 %fusion.65 = f32[768,1152]{1,0:T(8,128)} fusion(bf16[512,1152]{0,1:T(8,128)(2,1)} %bitcast.122, bf16[512,768]{1,0:T(8,128)(2,1)S(1)} %copy-done.4, f32[512]{0:T(512)S(1)} %get-tuple-element.32, f32[512]{0:T(512)S(1)} %get-tuple-element.31), kind=kOutput, calls=%fused_computation.75 | convolution fusion | flops 907542528 | bytes 5509120 | tf_op jit(solution)/shard_map/td,ta->da/dot_general | solution.py:113
  219.8 1.1 copy-done.1
  220.8 5.0 %fusion.12 = f32[1536,768]{1,0:T(8,128)} fusion(bf16[512,768]{1,0:T(8,128)(2,1)S(1)} %copy-done.1, bf16[512,1536]{1,0:T(8,128)(2,1)} %param.10), kind=kOutput, calls=%fused_computation.20 | convolution fusion | flops 1212678144 | bytes 7077888 | tf_op jit(solution)/shard_map/tf,td->fd/dot_general | solution.py:116
  226.0 5.3 %fusion.63 = f32[768,1536]{1,0:T(8,128)} fusion(bf16[512,1536]{1,0:T(8,128)(2,1)} %copy-done.6, bf16[512,768]{1,0:T(8,128)(2,1)} %param.8, f32[512]{0:T(512)S(1)} %get-tuple-element.32, f32[512]{0:T(512)S(1)} %get-tuple-element.31), kind=kOutput, calls=%fused_computation.73 | convolution fusion | flops 1209532416 | bytes 7081984 | tf_op jit(solution)/shard_map/td,tf->df/dot_general | solution.py:114
  231.4 2.6 fusion.11
  234.0 1.6 convert_bitcast_fusion.4
  235.6 20.7 %reduce-scatter.6.cloned.1.call-done = f32[64,768]{1,0:T(8,128)} async-done(((f32[512,768]{1,0:T(8,128)}), f32[64,768]{1,0:T(8,128)}) %reduce-scatter.6.cloned.1.call-update) | async-done | bytes 196624 | tf_op jit(solution)/shard_map/reduce_scatter | solution.py:96
  256.3 1.1 fusion.87
  257.5 20.6 %all-reduce = (f32[64]{0:T(128)S(1)}, f32[64]{0:T(128)S(1)}) all-reduce(f32[64]{0:T(128)S(1)} %get-tuple-element.22, f32[64]{0:T(128)S(1)} %get-tuple-element.21), channel_id=1, replica_groups=mesh['dp'=4,'row'=8,'col'=8] {'row'}, use_global_device_ids=true, to_apply=%region_20.0 | all-reduce | flops 128 | bytes 1024 | tf_op jit(solution)/shard_map/psum | solution.py:106
  278.1 1.8 add_convert_fusion
  279.9 19.6 %reduce-scatter.8.cloned.1.call-done = f32[192,1152]{1,0:T(8,128)} async-done(((f32[768,1152]{1,0:T(8,128)}), f32[192,1152]{1,0:T(8,128)}) %reduce-scatter.8.cloned.1.call-update) | async-done | bytes 884752 | tf_op jit(solution)/shard_map/reduce_scatter | solution.py:118
  299.4 1.2 convert_element_type.98
  300.8 0.8 copy.41
  301.6 53.3 %reduce-scatter.14.cloned.1.call-done = f32[384,768]{1,0:T(8,128)} async-done(((f32[1536,768]{1,0:T(8,128)}), f32[384,768]{1,0:T(8,128)}) %reduce-scatter.14.cloned.1.call-update) | async-done | bytes 1179664 | tf_op jit(solution)/shard_map/reduce_scatter | solution.py:121
  354.9 2.1 convert_bitcast_fusion.2
  357.0 53.5 %reduce-scatter.10.cloned.1.call-done = f32[192,1536]{1,0:T(8,128)} async-done(((f32[768,1536]{1,0:T(8,128)}), f32[192,1536]{1,0:T(8,128)}) %reduce-scatter.10.cloned.1.call-update) | async-done | bytes 1179664 | tf_op jit(solution)/shard_map/reduce_scatter | solution.py:119
  410.5 2.1 convert_bitcast_fusion.3
  (56 shorter events, 3.5 us)
Async XLA Ops:
  8.0 1.7 copy-start
  8.0 198.4 %all-reduce.5.cloned.1.call-start = ((), (), s32[]{:S(2)}) async-start(), calls=%async_computation.5 | async-start | bytes 6291456 | tf_op jit(solution)/shard_map/psum | solution.py:76
  13.9 220.1 %reduce-scatter.12.cloned.1.call-start = ((), (), s32[]{:S(2)}) async-start(), calls=%async_computation.9 | async-start | bytes 1474560 | tf_op jit(solution)/shard_map/reduce_scatter | solution.py:120
  21.0 4.1 copy-start.2
  31.9 224.5 %reduce-scatter.6.cloned.1.call-start = ((), (), s32[]{:S(2)}) async-start(), calls=%async_computation.6 | async-start | bytes 1769472 | tf_op jit(solution)/shard_map/reduce_scatter | solution.py:96
  31.9 2.9 copy-start.3
  125.2 4.8 %copy-start.9 = (f32[2,256,3,128]{1,3,2,0:T(8,128)S(1)}, f32[2,256,3,128]{1,3,2,0:T(8,128)}, u32[]{:S(2)}) copy-start(f32[2,256,3,128]{1,3,2,0:T(8,128)} %get-tuple-element.33) | copy-start | bytes 2359300
  125.2 4.8 %copy-start.11 = (f32[2,256,3]{1,2,0:T(4,128)S(1)}, f32[2,256,3]{1,2,0:T(4,128)}, u32[]{:S(2)}) copy-start(f32[2,256,3]{1,2,0:T(4,128)} %add_rsqrt_fusion) | copy-start | bytes 18436
  128.1 2.1 copy-start.8
  128.1 2.1 copy-start.10
  132.1 79.0 %copy-start.7 = (bf16[144,8,2,256]{3,1,2,0:T(8,128)(2,1)}, bf16[144,8,2,256]{3,1,2,0:T(8,128)(2,1)S(1)}, u32[]{:S(2)}) copy-start(bf16[144,8,2,256]{3,1,2,0:T(8,128)(2,1)S(1)} %copy.53) | copy-start | bytes 3538948
  206.4 3.2 copy-start.14
  209.6 1.4 copy-start.6
  209.6 2.0 copy-start.5
  214.1 0.7 copy-start.12
  214.1 0.7 copy-start.13
  214.1 1.1 copy-start.4
  214.1 85.3 %reduce-scatter.8.cloned.1.call-start = ((), (), s32[]{:S(2)}) async-start(), calls=%async_computation.7 | async-start | bytes 4423680 | tf_op jit(solution)/shard_map/reduce_scatter | solution.py:118
  219.7 1.1 copy-start.1
  219.7 135.1 %reduce-scatter.14.cloned.1.call-start = ((), (), s32[]{:S(2)}) async-start(), calls=%async_computation.10 | async-start | bytes 5898240 | tf_op jit(solution)/shard_map/reduce_scatter | solution.py:121
  225.9 184.6 %reduce-scatter.10.cloned.1.call-start = ((), (), s32[]{:S(2)}) async-start(), calls=%async_computation.8 | async-start | bytes 5898240 | tf_op jit(solution)/shard_map/reduce_scatter | solution.py:119
Sparse Core Ops, SparseCore 0:
  14.1 192.2 all-reduce.4
Sparse Core Ops, SparseCore 1:
  32.0 74.6 reduce-scatter.11
  214.2 42.1 reduce-scatter.5
  258.8 40.6 reduce-scatter.7
  302.0 52.8 reduce-scatter.13
  357.4 53.0 reduce-scatter.9
where the time goes:
time: 423 us; the launch traced here: 420 us
  waiting for transfers between devices  217 us (51%)
  blocking collectives  95 us (22%)
  matrix products  48.3 us (11%)
  local copies, waits for them, and re-layouts  21.8 us (5%)
  other arithmetic  21.7 us (5%)
  between operations  15.9 us (4%)
    psum x1, blocking collectives, body(): sum_attn, sum_hidden = lax.psum((part_attn, part_hidden), 'row')  74.5 us
    psum x1, waiting for transfers between devices, body(): sum_attn, sum_hidden = lax.psum((part_attn, part_hidden), 'row')  70.1 us
    reduce_scatter x1, waiting for transfers between devices, body(): lax.psum_scatter(part_up, 'dp', scatter_dimension=0, tiled=True)  53.5 us
    reduce_scatter x1, waiting for transfers between devices, body(): lax.psum_scatter(part_down, 'dp', scatter_dimension=0, tiled=True)  53.3 us
    reduce_scatter x1, waiting for transfers between devices, body(): lax.psum_scatter(total + jnp.einsum('tf,df->td', grad_pre, weight_up, pre...  20.7 us
    psum x1, blocking collectives, body(): lax.psum((jnp.sum(grad_normed, axis=1), jnp.sum(grad_normed * normed_shar...  20.6 us
    reduce_scatter x1, waiting for transfers between devices, body(): lax.psum_scatter(part_qkv, 'dp', scatter_dimension=0, tiled=True)  19.6 us
    unnamed x36, local copies, waits for them, and re-layouts  12.7 us
  transfers between devices with their start and end apart: 6, of which 5 were waited for; matrix products, arithmetic and copies ran while one was open for 19% of the time, Pallas kernels for 0%

commit v1 on v0

v1 whole, which is shorter than its diff:
```python
import jax
import jax.numpy as jnp
from jax import lax
from jax.experimental import pallas as pl
from jax.experimental.pallas import tpu as pltpu
from jax.sharding import PartitionSpec as P

MESH = pl.DeviceIdType.MESH
HD = 128
S = 256
EPS = 1e-06
SQRT_HALF = 0.7071067811865476
INV_ROOT_TWO_PI = 0.3989422804014327
F32 = jnp.float32
BF16 = jnp.bfloat16
N_COPIES = 69


def nt(a, b):
    return lax.dot_general(a, b, (((1,), (1,)), ((), ())), preferred_element_type=F32)


def tn(a, b):
    return lax.dot_general(a, b, (((0,), (0,)), ((), ())), preferred_element_type=F32)


def nn(a, b):
    return lax.dot_general(a, b, (((1,), (0,)), ((), ())), preferred_element_type=F32)


def gelu_exact(values):
    return 0.5 * values * (1.0 + lax.erf(values * SQRT_HALF))


def gelu_slope(values):
    cumul = 0.5 * (1.0 + lax.erf(values * SQRT_HALF))
    return cumul + values * jnp.exp(-0.5 * values * values) * INV_ROOT_TWO_PI


def head_norm(values):
    average = jnp.mean(values, axis=-1, keepdims=True)
    centred = values - average
    inv_std = lax.rsqrt(jnp.mean(centred * centred, axis=-1, keepdims=True) + EPS)
    return (centred * inv_std, inv_std)


def head_norm_back(normed, inv_std, upstream):
    first = jnp.mean(upstream, axis=-1, keepdims=True)
    cross = jnp.mean(upstream * normed, axis=-1, keepdims=True)
    return inv_std * (upstream - first - normed * cross)


def span(start, size):
    return pl.ds(pl.multiple_of(start, size), size)


def kernel(
    inp_h, qkv_h, up_h, cot_h, wqkv_h, wup_h, wattn_h, wdown_h,
    gin_o, gqkv_o, gup_o, gattn_o, gdown_o,
    inp, qkv, up, cot, wqkv, wup, wattn, wdown,
    stat_s, stat_r, stat_y,
    pa, pa_r, pay_s, pay_r,
    ph, phb, ph_r, phy_s, phy_r,
    go, gp, gf, hid, hid_s, att, n_t, n_p, probs_v, qn_v, kn_v,
    tot, zs, zr, fin_s, fin_r, fin_y,
    wgd, wga, wgq, wgu, ysd, yrd, ysa, yra, ysq, yrq, ysu, yru,
    load_sem, send_sem, recv_sem,
):
    dp, row, col = lax.axis_index("dp"), lax.axis_index("row"), lax.axis_index("col")
    y_lo, core = dp // 2, dp % 2
    x, y_hi = row // 2, row % 2
    width = 6144.0
    sib_dev = (y_lo * 2 + (1 - core), row, col)
    ylo_dev = ((1 - y_lo) * 2 + core, row, col)
    yhi_dev = (dp, x * 2 + (1 - y_hi), col)
    x_of = [(x + d) % 4 for d in (1, 2, 3)]
    x_dev = [(dp, xp * 2 + y_hi, col) for xp in x_of]
    z_of = [(col + d) % 8 for d in range(1, 8)]
    z_dev = [(dp, row, zp) for zp in z_of]

    loads = []
    for i, (src, dst) in enumerate([
        (cot_h, cot.at[0]), (wattn_h, wattn), (inp_h, inp), (wdown_h, wdown),
        (qkv_h, qkv), (up_h, up), (wqkv_h, wqkv), (wup_h, wup),
    ]):
        cp = pltpu.make_async_copy(src, dst, load_sem.at[i])
        cp.start()
        loads.append(cp)
    l_cot, l_wattn, l_inp, l_wdown, l_qkv, l_up, l_wqkv, l_wup = loads

    partners = [sib_dev, ylo_dev, yhi_dev] + x_dev + z_dev
    barrier = pltpu.get_barrier_semaphore()
    for dev in partners:
        pl.semaphore_signal(barrier, inc=1, device_id=dev, device_id_type=MESH)
    pl.semaphore_wait(barrier, len(partners))

    sent = []

    def push(src, dst, dev):
        i = len(sent)
        cp = pltpu.make_async_remote_copy(
            src, dst, send_sem.at[i], recv_sem.at[i], device_id=dev, device_id_type=MESH
        )
        cp.start()
        sent.append(cp)
        return cp

    l_inp.wait()
    stat_s[...] = jnp.zeros_like(stat_s)

    for g in range(4):
        block = inp[2 * g : 2 * g + 2].reshape(128, 768).astype(F32)
        block_t = block.T
        lanes = pl.ds(g * 128, 128)
        stat_s[0:1, lanes] = jnp.sum(block_t, axis=0, keepdims=True)
        stat_s[1:2, lanes] = jnp.sum(block_t * block_t, axis=0, keepdims=True)
        n_t[:, lanes] = block_t.astype(BF16)
    c_stat = [push(stat_s, stat_r.at[d], x_dev[d]) for d in range(3)]

    l_cot.wait()
    l_wattn.wait()
    c_cot = push(cot.at[0], cot.at[1], sib_dev)

    @pl.loop(0, 2)
    def _(b):
        acc = nt(cot[0, pl.ds(b * 4, 4)].reshape(256, 768), wattn[...])
        pa[pl.ds(b * 4, 4)] = acc.reshape(4, 2, 32, 384)

    c_pa = [push(pa.at[pl.ds(2 * x_of[d], 2)], pa_r.at[d], x_dev[d]) for d in range(3)]

    l_wdown.wait()
    c_ph = []
    for p in range(2):
        @pl.loop(0, 6)
        def _(n):
            cols = span(n * 256, 256)
            acc = nt(cot[0, :, p].reshape(256, 768), wdown[cols, :]).reshape(8, 32, 256)
            ph[:, p, :, cols] = acc
            phb[:, p, :, cols] = acc.astype(BF16)

        c_ph.append([
            push(phb.at[pl.ds(2 * x_of[d], 2), p], ph_r.at[p, d], x_dev[d]) for d in range(3)
        ])

    l_up.wait()
    for s in range(4):
        @pl.loop(0, 8)
        def _(r):
            hid[s, r] = gelu_exact(up[r, :, :, s * 384 : (s + 1) * 384].astype(F32)).astype(BF16)

    c_hid = [push(hid.at[2 * j + 1 - core], hid_s.at[j], sib_dev) for j in range(2)]

    for cp in c_stat:
        cp.wait_recv()
    stat_y[...] = stat_s[...] + stat_r[0] + stat_r[1] + stat_r[2]
    c_staty = push(stat_y, stat_r.at[3], yhi_dev)

    l_qkv.wait()
    scale = HD ** (-0.5)

    @pl.loop(0, 6)
    def _(i):
        b, h = i // 3, i % 3
        rows = span(b * 256, 256)
        lanes = span(h * 128, 128)
        qn, _ = head_norm(qkv[rows, lanes].astype(F32))
        kn, _ = head_norm(qkv[rows, span(384 + h * 128, 128)].astype(F32))
        qn_b = qn.astype(BF16)
        kn_b = kn.astype(BF16)
        qn_v[rows, lanes] = qn_b
        kn_v[rows, lanes] = kn_b
        expo = jnp.exp(nt(qn_b, kn_b) * scale)
        probs = expo / jnp.sum(expo, axis=-1, keepdims=True)
        probs_v[i] = probs
        att[0, rows, lanes] = nn(
            probs.astype(BF16), qkv[rows, span(768 + h * 128, 128)]
        ).astype(BF16)

    c_att = push(att.at[0], att.at[1], sib_dev)

    own = x * 2 + y_hi
    other = x * 2 + (1 - y_hi)
    for cp in c_pa:
        cp.wait_recv()
    pay_s[...] = pa[other] + pa_r[0, 1 - y_hi] + pa_r[1, 1 - y_hi] + pa_r[2, 1 - y_hi]
    c_pay = push(pay_s, pay_r, yhi_dev)
    part_o = pa[own] + pa_r[0, y_hi] + pa_r[1, y_hi] + pa_r[2, y_hi]

    c_staty.wait_recv()
    stat = stat_y[...] + stat_r[3]
    mean_r = stat[0:1] / width
    inv_r = lax.rsqrt(stat[1:2] / width - mean_r * mean_r + EPS)

    @pl.loop(0, 8)
    def _(k):
        rows = span(k * 96, 96)
        n_t[rows, :] = ((n_t[rows, :].astype(F32) - mean_r) * inv_r).astype(BF16)

    c_nt = [
        push(n_t.at[span((2 * j + 1 - core) * 192, 192)], n_p.at[j, :, pl.ds(512, 512)], sib_dev)
        for j in range(2)
    ]
    l_nt = []
    for j in range(2):
        cp = pltpu.make_async_copy(
            n_t.at[span((2 * j + core) * 192, 192)], n_p.at[j, :, pl.ds(0, 512)], load_sem.at[8 + j]
        )
        cp.start()
        l_nt.append(cp)

    c_pay.wait_recv()
    go[own] = (part_o + pay_r[...]).astype(BF16)
    c_goy = push(go.at[own], go.at[own], yhi_dev)
    c_go = [push(go.at[own], go.at[own], dev) for dev in x_dev]

    def hidden_sum(p):
        for cp in c_ph[p]:
            cp.wait_recv()
        o = 1 - y_hi
        phy_s[p] = (
            ph[other, p] + ph_r[p, 0, o].astype(F32) + ph_r[p, 1, o].astype(F32)
            + ph_r[p, 2, o].astype(F32)
        )
        return push(phy_s.at[p], phy_r.at[p], yhi_dev)

    def hidden_slope(p, cp):
        part = (
            ph[own, p] + ph_r[p, 0, y_hi].astype(F32) + ph_r[p, 1, y_hi].astype(F32)
            + ph_r[p, 2, y_hi].astype(F32)
        )
        slope = gelu_slope(up[own, p].astype(F32))
        cp.wait_recv()
        gp[0, own, p] = ((part + phy_r[p]) * slope).astype(BF16)
        here = gp.at[0, own, p]
        return push(here, here, yhi_dev), [push(here, here, dev) for dev in x_dev]

    def relay(cp, ref):
        cp.wait_recv()
        return [push(ref, ref, dev) for dev in x_dev]

    c_cot.wait_recv()
    for cp in c_hid:
        cp.wait_recv()
    y_other = 1 - y_lo

    def down(j):
        @pl.loop(0, 3)
        def _(n):
            cols = span(n * 256, 256)
            acc = tn(hid[2 * j + core].reshape(512, 384), cot[0, :, :, :, cols].reshape(512, 256))
            acc += tn(hid_s[j].reshape(512, 384), cot[1, :, :, :, cols].reshape(512, 256))
            wgd[j, :, cols] = acc

    down(y_other)
    ysd[...] = wgd[y_other].astype(BF16)
    c_d = push(ysd, yrd, ylo_dev)
    c_phy0 = hidden_sum(0)
    c_gof = relay(c_goy, go.at[other])
    down(y_lo)
    c_gpy0, c_gp0 = hidden_slope(0, c_phy0)

    c_att.wait_recv()

    @pl.loop(0, 3)
    def _(n):
        cols = span(n * 256, 256)
        acc = tn(att[0], cot[0, :, :, :, cols].reshape(512, 256))
        acc += tn(att[1], cot[1, :, :, :, cols].reshape(512, 256))
        wga[:, cols] = acc

    ysa[...] = wga[span((2 * y_other + core) * 96, 96), :].astype(BF16)
    c_a = push(ysa, yra, ylo_dev)

    c_gpf0 = relay(c_gpy0, gp.at[0, other, 0])
    c_phy1 = hidden_sum(1)

    for cp in c_go + c_gof:
        cp.wait_recv()

    @pl.loop(0, 6)
    def _(i):
        b, h = i // 3, i % 3
        rows = span(b * 256, 256)
        lanes = span(h * 128, 128)
        lanes_k = span(384 + h * 128, 128)
        lanes_v = span(768 + h * 128, 128)
        grad_o = go[pl.ds(b * 4, 4), :, :, lanes].reshape(256, 128)
        probs = probs_v[i]
        probs_b = probs.astype(BF16)
        grad_probs = nt(grad_o, qkv[rows, lanes_v])
        gf[0, rows, lanes_v] = tn(probs_b, grad_o).astype(BF16)
        rowdot = jnp.sum(probs * grad_probs, axis=-1, keepdims=True)
        grad_scores = (probs * (grad_probs - rowdot) * scale).astype(BF16)
        q_norm, q_inv = head_norm(qkv[rows, lanes].astype(F32))
        grad_qn = nn(grad_scores, kn_v[rows, lanes])
        gf[0, rows, lanes] = head_norm_back(q_norm, q_inv, grad_qn).astype(BF16)
        k_norm, k_inv = head_norm(qkv[rows, lanes_k].astype(F32))
        grad_kn = tn(grad_scores, qn_v[rows, lanes])
        gf[0, rows, lanes_k] = head_norm_back(k_norm, k_inv, grad_kn).astype(BF16)

    c_gf = push(gf.at[0], gf.at[1], sib_dev)
    c_gpy1, c_gp1 = hidden_slope(1, c_phy1)

    l_wqkv.wait()

    @pl.loop(0, 6)
    def _(i):
        b, n = i // 3, i % 3
        cols = span(n * 256, 256)
        acc = nt(gf[0, span(b * 256, 256), :], wqkv[cols, :])
        tot[pl.ds(b * 4, 4), :, :, cols] = acc.reshape(4, 2, 32, 256)

    c_gpf1 = relay(c_gpy1, gp.at[0, other, 1])

    c_gf.wait_recv()
    for cp in c_nt:
        cp.wait_recv()
    for cp in l_nt:
        cp.wait()

    @pl.loop(0, 3)
    def _(n):
        cols = span(n * 384, 384)
        acc = nn(n_p[...].reshape(384, 1024), gf[:, :, cols].reshape(1024, 384))
        wgq[:, :, cols] = acc.reshape(2, 192, 384)

    ysq[...] = wgq[y_other].astype(BF16)
    c_q = push(ysq, yrq, ylo_dev)

    l_wup.wait()
    c_z = []
    c_gps = []
    for p, waits in ((0, c_gp0 + c_gpf0), (1, c_gp1 + c_gpf1)):
        for cp in waits:
            cp.wait_recv()
        c_gps.append(push(gp.at[0, :, p], gp.at[1, :, p], sib_dev))

        @pl.loop(0, 3)
        def _(n):
            cols = span(n * 256, 256)
            acc = nt(gp[0, :, p].reshape(256, 1536), wup[cols, :]).reshape(8, 32, 256)
            acc = acc + tot[:, p, :, cols]
            tot[:, p, :, cols] = acc
            zs[p, :, :, cols] = acc.astype(BF16)

        c_z.append([push(zs.at[p, z_of[d]], zr.at[p, d], z_dev[d]) for d in range(7)])

    for cp in c_gps:
        cp.wait_recv()
    c_u = []
    for half in range(2):
        @pl.loop(0, 3)
        def _(n):
            cols = span(half * 768 + n * 256, 256)
            acc = nn(n_p[...].reshape(384, 1024), gp[:, :, :, :, cols].reshape(1024, 256))
            wgu[half, :, :, span(n * 256, 256)] = acc.reshape(2, 192, 256)

        ysu[half] = wgu[half, y_other].astype(BF16)
        c_u.append(push(ysu.at[half], yru.at[half], ylo_dev))

    lane = lax.broadcasted_iota(jnp.int32, (64, 512), 1)
    token = lax.broadcasted_iota(jnp.int32, (64, 512), 0)
    pick = jnp.where(lane == token + col * 64, 1.0, 0.0).astype(F32)
    mean_c = jnp.sum(pick * mean_r, axis=1, keepdims=True)
    inv_c = jnp.sum(pick * inv_r, axis=1, keepdims=True)
    normed = (inp[col].reshape(64, 768).astype(F32) - mean_c) * inv_c
    gn = []
    for p in range(2):
        for cp in c_z[p]:
            cp.wait_recv()
        value = tot[col, p]
        for d in range(7):
            value = value + zr[p, d].astype(F32)
        gn.append(value)
    grad_n = jnp.concatenate(gn, axis=0)
    sum_g = jnp.sum(grad_n, axis=1, keepdims=True)
    sum_c = jnp.sum(grad_n * normed, axis=1, keepdims=True)
    lane = lax.broadcasted_iota(jnp.int32, (64, 128), 1)
    token = lax.broadcasted_iota(jnp.int32, (64, 128), 0)
    eye = jnp.where(lane == token, 1.0, 0.0).astype(F32)
    fin_s[...] = jnp.zeros_like(fin_s)
    fin_s[0:1, :] = jnp.sum(eye * sum_g, axis=0, keepdims=True)
    fin_s[1:2, :] = jnp.sum(eye * sum_c, axis=0, keepdims=True)
    c_fin = [push(fin_s, fin_r.at[d], x_dev[d]) for d in range(3)]

    c_d.wait_recv()
    gdown_o[...] = (wgd[y_lo] + yrd[...].astype(F32)).astype(BF16)
    c_a.wait_recv()
    gattn_o[...] = (
        wga[span((2 * y_lo + core) * 96, 96), :] + yra[...].astype(F32)
    ).astype(BF16)

    for cp in c_fin:
        cp.wait_recv()
    fin_y[...] = fin_s[...] + fin_r[0] + fin_r[1] + fin_r[2]
    c_finy = push(fin_y, fin_r.at[3], yhi_dev)

    c_q.wait_recv()
    gqkv_o[...] = (wgq[y_lo] + yrq[...].astype(F32)).astype(BF16)

    c_finy.wait_recv()
    fin = fin_y[...] + fin_r[3]
    mean_g = jnp.sum(eye * fin[0:1], axis=1, keepdims=True) / width
    mean_x = jnp.sum(eye * fin[1:2], axis=1, keepdims=True) / width
    branch = grad_n - mean_g - normed * mean_x
    result = cot[0, col].reshape(64, 768).astype(F32) + inv_c * branch
    gin_o[...] = result.astype(BF16)

    for half in range(2):
        c_u[half].wait_recv()
        gup_o[:, half * 768 : (half + 1) * 768] = (
            wgu[half, y_lo] + yru[half].astype(F32)
        ).astype(BF16)

    for cp in sent:
        cp.wait_send()
    assert len(sent) == N_COPIES, len(sent)


def body(inputs, saved_qkv, saved_up, cotangent, weight_qkv, weight_up, weight_attn, weight_down):
    vm = pltpu.VMEM
    scratch = [
        vm((8, 2, 32, 768), BF16), vm((512, 1152), BF16), vm((8, 2, 32, 1536), BF16),
        vm((2, 8, 2, 32, 768), BF16),
        vm((768, 1152), BF16), vm((768, 1536), BF16), vm((384, 768), BF16), vm((1536, 768), BF16),
        vm((8, 512), F32), vm((4, 8, 512), F32), vm((8, 512), F32),
        vm((8, 2, 32, 384), F32), vm((3, 2, 2, 32, 384), F32),
        vm((2, 32, 384), F32), vm((2, 32, 384), F32),
        vm((8, 2, 32, 1536), F32), vm((8, 2, 32, 1536), BF16), vm((2, 3, 2, 32, 1536), BF16),
        vm((2, 32, 1536), F32), vm((2, 32, 1536), F32),
        vm((8, 2, 32, 384), BF16), vm((2, 8, 2, 32, 1536), BF16), vm((2, 512, 1152), BF16),
        vm((4, 8, 2, 32, 384), BF16), vm((2, 8, 2, 32, 384), BF16), vm((2, 512, 384), BF16),
        vm((768, 512), BF16), vm((2, 192, 1024), BF16),
        vm((6, 256, 256), F32), vm((512, 384), BF16), vm((512, 384), BF16),
        vm((8, 2, 32, 768), F32), vm((2, 8, 32, 768), BF16), vm((2, 7, 32, 768), BF16),
        vm((8, 128), F32), vm((4, 8, 128), F32), vm((8, 128), F32),
        vm((2, 384, 768), F32), vm((384, 768), F32), vm((2, 192, 1152), F32),
        vm((2, 2, 192, 768), F32),
        vm((384, 768), BF16), vm((384, 768), BF16), vm((96, 768), BF16), vm((96, 768), BF16),
        vm((192, 1152), BF16), vm((192, 1152), BF16),
        vm((2, 192, 768), BF16), vm((2, 192, 768), BF16),
        pltpu.SemaphoreType.DMA((10,)),
        pltpu.SemaphoreType.DMA((N_COPIES,)),
        pltpu.SemaphoreType.DMA((N_COPIES,)),
    ]
    gin, gqkv, gup, gattn, gdown = pl.pallas_call(
        kernel,
        out_shape=(
            jax.ShapeDtypeStruct((64, 768), BF16),
            jax.ShapeDtypeStruct((192, 1152), BF16),
            jax.ShapeDtypeStruct((192, 1536), BF16),
            jax.ShapeDtypeStruct((96, 768), BF16),
            jax.ShapeDtypeStruct((384, 768), BF16),
        ),
        in_specs=[pl.BlockSpec(memory_space=pl.ANY)] * 8,
        out_specs=[pl.BlockSpec(memory_space=pltpu.VMEM)] * 5,
        scratch_shapes=scratch,
        compiler_params=pltpu.CompilerParams(
            collective_id=0, has_side_effects=True, vmem_limit_bytes=58 * 2**20
        ),
        name="layer_backward",
    )(
        inputs.reshape(8, 2, 32, 768),
        saved_qkv.reshape(512, 1152),
        saved_up.reshape(8, 2, 32, 1536),
        cotangent.reshape(8, 2, 32, 768),
        weight_qkv.reshape(768, 1152),
        weight_up,
        weight_attn,
        weight_down,
    )
    return (
        gin,
        gqkv.reshape(1, 1, 192, 3, 384),
        gup.reshape(1, 1, 192, 1536),
        gattn.reshape(1, 1, 96, 768),
        gdown.reshape(1, 1, 384, 768),
    )


def solution(mesh):
    return jax.shard_map(
        body,
        mesh=mesh,
        in_specs=(
            P("dp", "row"),
            P("dp", None, "col"),
            P("dp", "col"),
            P("dp", "row"),
            P("row", None, "col"),
            P("row", "col"),
            P("col", "row"),
            P("col", "row"),
        ),
        out_specs=(
            P(("dp", "col"), "row"),
            P("row", "dp", None, None, "col"),
            P("row", "dp", None, "col"),
            P("col", "dp", None, "row"),
            P("col", "dp", None, "row"),
        ),
        check_vma=False,
    )
```

time: 423 us -> 105 us (0.25)
  waiting for transfers between devices: 217 us -> 0 us
  blocking collectives: 95 us -> 0 us
  Pallas kernels: 0 us -> 91.9 us
  matrix products: 48.3 us -> 0 us
  other arithmetic: 21.7 us -> 0 us
  between operations: 15.9 us -> 0.71 us
  local copies, waits for them, and re-layouts: 21.8 us -> 12 us
    reduce_scatter x5 -> x0, waiting for transfers between devices: 147 us -> none  [the longest x1 53.5 us: body(): lax.psum_scatter(part_up, 'dp', scatter_dimension=0, tiled=True)]
    psum x2 -> x0, blocking collectives: 95 us -> none  [the longest x1 74.5 us: body(): sum_attn, sum_hidden = lax.psum((part_attn, part_hidden), 'row')]
    pallas_call x0 -> x1, Pallas kernels: none -> 91.9 us  [body(): pl.pallas_call(kernel, out_shape=(jax.ShapeDtypeStruct((64, 768), BF16),...]
    psum x1 -> x0, waiting for transfers between devices: 70.1 us -> none  [body(): sum_attn, sum_hidden = lax.psum((part_attn, part_hidden), 'row')]
    dot_general x13 -> x0, matrix products: 45.8 us -> none  [the longest x1 5.35 us: body(): jnp.einsum('td,tf->df', normed_b, grad_pre, preferred_element_type=f32)]
    convert_element_type x3 -> x0, other arithmetic: 6.17 us -> none  [the longest x1 3.17 us: body(): grad_pre = (sum_hidden * gelu_slope(saved_up.astype(f32))).astype(bf16)]
    reshape x3 -> x0, other arithmetic: 5.93 us -> none  [the longest x1 2.14 us: body(): grad_up = summed_up.astype(bf16).reshape(1, 1, summed_up.shape[0], up_cols)]
    unnamed x36 -> x17, local copies, waits for them, and re-layouts: 12.7 us -> 6.76 us
  transfers between devices with their start and end apart: 6 -> 0, of which waited for: 5 -> 0; matrix products, arithmetic and copies ran while one was open for 19% -> 0% of each run, Pallas kernels for 0% -> 0%
where the time goes in v1:
time: 105 us
  Pallas kernels  91.9 us (88%)
  local copies, waits for them, and re-layouts  12 us (11%)
    pallas_call x1, Pallas kernels, body(): pl.pallas_call(kernel, out_shape=(jax.ShapeDtypeStruct((64, 768), BF16),...  91.9 us
    unnamed x17, local copies, waits for them, and re-layouts  6.76 us
    reshape x1, local copies, waits for them, and re-layouts, body(): weight_qkv.reshape(768, 1152)  2.25 us

profile of v1, /device:TPU:24, one launch (start us, length us, event | category | flops | bytes accessed | tf_op | source)
XLA Modules:
  0.0 104.6 jit_solution(13079701970523799745)
XLA Ops:
  0.6 1.6 %copy.16 = bf16[512,3,384]{0,2,1:T(8,128)(2,1)S(1)} copy(bf16[512,3,384]{2,0,1:T(8,128)(2,1)} %param.9) | data formatting | bytes 2359296 | tf_op args[1]
  2.2 0.0 copy-start
  2.2 1.4 %copy.18.qkv_h = bf16[512,1152]{1,0:T(8,128)(2,1)} copy(bf16[512,1152]{0,1:T(8,128)(2,1)S(1)} %bitcast.9) | data formatting | bytes 2359296 | tf_op jit(solution)/shard_map/reshape | solution.py:464
  3.6 0.5 copy-done
  4.1 0.9 copy.17
  5.1 2.3 %copy.19.wqkv_h = bf16[768,1152]{1,0:T(8,128)(2,1)} copy(bf16[768,1152]{0,1:T(8,128)(2,1)S(1)} %bitcast.8) | data formatting | bytes 3538944 | tf_op jit(solution)/shard_map/reshape | solution.py:467
  7.3 91.9 %layer_backward.1 = (bf16[64,768]{1,0:T(8,128)(2,1)}, bf16[192,1152]{1,0:T(8,128)(2,1)}, bf16[192,1536]{1,0:T(8,128)(2,1)}, bf16[96,768]{1,0:T(8,128)(2,1)}, bf16[384,768]{1,0:T(8,128)(2,1)}) custom-call(bf16[8,2,32,768]{3,2,1,0:T(8,128)(2,1)} %bitcast.11, bf16[512,1152]{1,0:T(8,128)(2,1)} %copy.18.qkv_h, bf16[8,2,32,1536]{3,2,1,0:T(8,128)(2,1)} %bitcast.10, ...), custom_call_target="tpu_custom_call" | custom-call | tf_op jit(solution)/shard_map/layer_backward/pallas_call | solution.py:446
  99.2 0.0 copy-start.4
  99.3 0.0 copy-start.2
  99.3 0.0 copy-start.3
  99.3 0.0 copy-start.1
  99.3 1.5 %reshape.42 = bf16[1,1,192,3,384]{4,3,2,1,0:T(4,128)(2,1)S(1)} reshape(bf16[192,1152]{1,0:T(8,128)(2,1)} %get-tuple-element.11) | data formatting | bytes 884736 | tf_op jit(solution)/shard_map/reshape | solution.py:474
  100.8 0.8 copy.20
  101.7 0.0 copy-done.4
  101.7 0.6 copy.25
  102.3 0.0 copy-done.2
  102.3 0.8 copy.26
  103.1 0.0 copy-done.3
  103.1 0.7 copy.27
  103.8 0.0 copy-done.1
  103.8 0.8 copy.28
Async XLA Ops:
  2.2 1.9 %copy-start = (bf16[768,3,384]{2,0,1:T(8,128)(2,1)S(1)}, bf16[768,3,384]{2,0,1:T(8,128)(2,1)}, u32[]{:S(2)}) copy-start(bf16[768,3,384]{2,0,1:T(8,128)(2,1)} %param.12) | copy-start | bytes 5308420
  99.2 2.4 %copy-start.4 = (bf16[64,768]{1,0:T(8,128)(2,1)S(1)}, bf16[64,768]{1,0:T(8,128)(2,1)}, u32[]{:S(2)}) copy-start(bf16[64,768]{1,0:T(8,128)(2,1)} %get-tuple-element.30) | copy-start | bytes 294916
  99.3 3.0 %copy-start.2 = (bf16[192,1536]{1,0:T(8,128)(2,1)S(1)}, bf16[192,1536]{1,0:T(8,128)(2,1)}, u32[]{:S(2)}) copy-start(bf16[192,1536]{1,0:T(8,128)(2,1)} %get-tuple-element.12) | copy-start | bytes 1769476
  99.3 3.9 %copy-start.3 = (bf16[96,768]{1,0:T(8,128)(2,1)S(1)}, bf16[96,768]{1,0:T(8,128)(2,1)}, u32[]{:S(2)}) copy-start(bf16[96,768]{1,0:T(8,128)(2,1)} %get-tuple-element.13) | copy-start | bytes 442372
  99.3 4.5 %copy-start.1 = (bf16[384,768]{1,0:T(8,128)(2,1)S(1)}, bf16[384,768]{1,0:T(8,128)(2,1)}, u32[]{:S(2)}) copy-start(bf16[384,768]{1,0:T(8,128)(2,1)} %get-tuple-element.14) | copy-start | bytes 1769476

commit v2 on v1

v2 whole, which is shorter than its diff:
```python
import jax
import jax.numpy as jnp
from jax import lax
from jax.experimental import pallas as pl
from jax.experimental.pallas import tpu as pltpu
from jax.sharding import PartitionSpec as P

MESH = pl.DeviceIdType.MESH
HD = 128
S = 256
EPS = 1e-06
SQRT_HALF = 0.7071067811865476
INV_ROOT_TWO_PI = 0.3989422804014327
F32 = jnp.float32
BF16 = jnp.bfloat16
N_COPIES = 85


def nt(a, b):
    return lax.dot_general(a, b, (((1,), (1,)), ((), ())), preferred_element_type=F32)


def tn(a, b):
    return lax.dot_general(a, b, (((0,), (0,)), ((), ())), preferred_element_type=F32)


def nn(a, b):
    return lax.dot_general(a, b, (((1,), (0,)), ((), ())), preferred_element_type=F32)


def gelu_exact(values):
    return 0.5 * values * (1.0 + lax.erf(values * SQRT_HALF))


def gelu_slope(values):
    cumul = 0.5 * (1.0 + lax.erf(values * SQRT_HALF))
    return cumul + values * jnp.exp(-0.5 * values * values) * INV_ROOT_TWO_PI


def head_norm(values):
    average = jnp.mean(values, axis=-1, keepdims=True)
    centred = values - average
    inv_std = lax.rsqrt(jnp.mean(centred * centred, axis=-1, keepdims=True) + EPS)
    return (centred * inv_std, inv_std)


def head_norm_back(normed, inv_std, upstream):
    first = jnp.mean(upstream, axis=-1, keepdims=True)
    cross = jnp.mean(upstream * normed, axis=-1, keepdims=True)
    return inv_std * (upstream - first - normed * cross)


def span(start, size):
    return pl.ds(pl.multiple_of(start, size), size)


def kernel(
    inp_h, qkv_h, up_h, cot_h, wqkv_h, wup_h, wattn_h, wdown_h,
    gin_o, gqkv_o, gup_o, gattn_o, gdown_o,
    inp, qkv, up, cot, wqkv, wup, wattn, wdown,
    stat_s, stat_r, stat_y,
    pa, pa_r, pay_s, pay_r,
    ph, phb, ph_r, phx, phy_s, phy_r,
    go, gp, gf, hid, hid_s, att, n_t, n_p, probs_v, qn_v, kn_v,
    tot, zs, zr, fin_s, fin_r, fin_y,
    wgd, wga, wgq, wgu, ysd, yrd, ysa, yra, ysq, yrq, ysu, yru,
    load_sem, send_sem, recv_sem,
):
    dp, row, col = lax.axis_index("dp"), lax.axis_index("row"), lax.axis_index("col")
    y_lo, core = dp // 2, dp % 2
    x, y_hi = row // 2, row % 2
    y_other = 1 - y_lo
    width = 6144.0
    scale = HD ** (-0.5)
    x_next, x_far, x_prev = (x + 1) % 4, (x + 2) % 4, (x + 3) % 4
    sib_dev = (y_lo * 2 + (1 - core), row, col)
    ylo_dev = (y_other * 2 + core, row, col)
    yhi_dev = (dp, x * 2 + (1 - y_hi), col)
    next_dev = (dp, x_next * 2 + y_hi, col)
    far_dev = (dp, x_far * 2 + y_hi, col)
    prev_dev = (dp, x_prev * 2 + y_hi, col)
    x_dev = [next_dev, far_dev, prev_dev]
    z_of = [(col + d) % 8 for d in range(1, 8)]
    z_dev = [(dp, row, zp) for zp in z_of]

    def load(i, src, dst):
        cp = pltpu.make_async_copy(src, dst, load_sem.at[i])
        cp.start()
        return cp

    l_cot = load(0, cot_h, cot.at[0])
    l_wattn = load(1, wattn_h, wattn)

    partners = [sib_dev, ylo_dev, yhi_dev] + x_dev + z_dev
    barrier = pltpu.get_barrier_semaphore()
    for dev in partners:
        pl.semaphore_signal(barrier, inc=1, device_id=dev, device_id_type=MESH)

    sent = []

    def push(src, dst, dev):
        i = len(sent)
        cp = pltpu.make_async_remote_copy(
            src, dst, send_sem.at[i], recv_sem.at[i], device_id=dev, device_id_type=MESH
        )
        cp.start()
        sent.append(cp)
        return cp

    x_of = [x_next, x_far, x_prev]

    def scatter(block, land):
        return [push(block(x_of[d]), land.at[d], x_dev[d]) for d in range(3)]

    def gather(chunk):
        cps = []
        for dev in (next_dev, prev_dev):
            for i in range(2):
                ref = chunk(2 * x + i)
                cps.append(push(ref, ref, dev))
        return cps

    def gather_far(chunk, cps):
        cps[0].wait_recv()
        ref = chunk(2 * x_prev)
        cps.append(push(ref, ref, next_dev))
        cps[3].wait_recv()
        ref = chunk(2 * x_next + 1)
        cps.append(push(ref, ref, prev_dev))

    def gather_end(cps):
        for i in (1, 2, 4, 5):
            cps[i].wait_recv()

    l_cot.wait()
    l_wattn.wait()

    @pl.loop(0, 2)
    def _(b):
        acc = nt(cot[0, pl.ds(b * 4, 4)].reshape(256, 768), wattn[...])
        pa[pl.ds(b * 4, 4)] = acc.reshape(4, 2, 32, 384)

    l_up = load(2, up_h, up)
    l_wdown = load(3, wdown_h, wdown)
    l_qkv = load(4, qkv_h, qkv)
    l_inp = load(5, inp_h, inp)

    def activate(y):
        @pl.loop(0, 16)
        def _(i):
            r, s = i // 2, 2 * y + i % 2
            hid[s, r] = gelu_exact(up[r, :, :, span(s * 384, 384)].astype(F32)).astype(BF16)

    pl.semaphore_wait(barrier, len(partners))
    c_pa = scatter(lambda xp: pa.at[pl.ds(2 * xp, 2)], pa_r)
    c_cot = push(cot.at[0], cot.at[1], sib_dev)
    l_up.wait()
    activate(y_other)
    c_hid = [push(hid.at[2 * y_other + 1 - core], hid_s.at[y_other], sib_dev)]
    l_wdown.wait()
    l_wqkv = load(6, wqkv_h, wqkv)
    l_wup = load(7, wup_h, wup)

    def hidden_start(c, p):
        @pl.loop(0, 3)
        def _(n):
            cols = span(n * 256, 256)
            acc = nt(
                cot[0, :, p].reshape(256, 768), wdown[span(c * 768 + n * 256, 256), :]
            ).reshape(8, 32, 256)
            ph[c, :, p, :, cols] = acc
            phb[c, :, p, :, cols] = acc.astype(BF16)

        return scatter(lambda xp: phb.at[c, pl.ds(2 * xp, 2), p], ph_r.at[c, p])

    def hidden_sum(c, p, cps):
        for cp in cps:
            cp.wait_recv()
        total = ph[c, pl.ds(2 * x, 2), p]
        for d in range(3):
            total = total + ph_r[c, p, d].astype(F32)
        phx[c, p] = total
        phy_s[c, p] = total.astype(BF16)
        return push(phy_s.at[c, p], phy_r.at[c, p], yhi_dev)

    def hidden_chunk(c, p):
        return lambda r: gp.at[0, c, r, p]

    def hidden_slope(c, p, cp):
        slope = gelu_slope(up[pl.ds(2 * x, 2), p, :, c * 768 : (c + 1) * 768].astype(F32))
        cp.wait_recv()
        gp[0, c, pl.ds(2 * x, 2), p] = (
            (phx[c, p] + phy_r[c, p].astype(F32)) * slope
        ).astype(BF16)
        return gather(hidden_chunk(c, p))

    def down(j):
        @pl.loop(0, 3)
        def _(n):
            cols = span(n * 256, 256)
            acc = tn(hid[2 * j + core].reshape(512, 384), cot[0, :, :, :, cols].reshape(512, 256))
            acc += tn(hid_s[j].reshape(512, 384), cot[1, :, :, :, cols].reshape(512, 256))
            wgd[j, :, cols] = acc

    def attention(b):
        @pl.loop(0, 3)
        def _(h):
            rows = pl.ds(b * 256, 256)
            lanes = span(h * 128, 128)
            qn, _ = head_norm(qkv[0, rows, lanes].astype(F32))
            kn, _ = head_norm(qkv[1, rows, lanes].astype(F32))
            qn_b = qn.astype(BF16)
            kn_b = kn.astype(BF16)
            qn_v[rows, lanes] = qn_b
            kn_v[rows, lanes] = kn_b
            expo = jnp.exp(nt(qn_b, kn_b) * scale)
            probs = expo / jnp.sum(expo, axis=-1, keepdims=True)
            probs_v[b * 3 + h] = probs
            att[0, rows, lanes] = nn(probs.astype(BF16), qkv[2, rows, lanes]).astype(BF16)

    def attention_back(b):
        @pl.loop(0, 3)
        def _(h):
            rows = pl.ds(b * 256, 256)
            lanes = span(h * 128, 128)
            grad_o = go[pl.ds(b * 4, 4), :, :, lanes].reshape(256, 128)
            probs = probs_v[b * 3 + h]
            probs_b = probs.astype(BF16)
            grad_probs = nt(grad_o, qkv[2, rows, lanes])
            gf[0, 2, rows, lanes] = tn(probs_b, grad_o).astype(BF16)
            rowdot = jnp.sum(probs * grad_probs, axis=-1, keepdims=True)
            grad_scores = (probs * (grad_probs - rowdot) * scale).astype(BF16)
            q_norm, q_inv = head_norm(qkv[0, rows, lanes].astype(F32))
            grad_qn = nn(grad_scores, kn_v[rows, lanes])
            gf[0, 0, rows, lanes] = head_norm_back(q_norm, q_inv, grad_qn).astype(BF16)
            k_norm, k_inv = head_norm(qkv[1, rows, lanes].astype(F32))
            grad_kn = tn(grad_scores, qn_v[rows, lanes])
            gf[0, 1, rows, lanes] = head_norm_back(k_norm, k_inv, grad_kn).astype(BF16)

    def share(c, p):
        gather_end(c_gp[c, p])
        return push(gp.at[0, c, :, p], gp.at[1, c, :, p], sib_dev)

    c_ph = {}
    c_ph[0, 0] = hidden_start(0, 0)

    c_cot.wait_recv()
    c_hid[0].wait_recv()
    down(y_other)
    ysd[...] = wgd[y_other].astype(BF16)
    c_d = push(ysd, yrd, ylo_dev)

    c_ph[0, 1] = hidden_start(0, 1)
    c_ph[1, 0] = hidden_start(1, 0)
    c_ph[1, 1] = hidden_start(1, 1)

    l_qkv.wait()
    attention(0)

    mine = pl.ds(2 * x, 2)
    for cp in c_pa:
        cp.wait_recv()
    pay_s[...] = pa[mine] + pa_r[0] + pa_r[1] + pa_r[2]
    c_pay = push(pay_s, pay_r, yhi_dev)

    attention(1)
    c_att = push(att.at[0], att.at[1], sib_dev)

    l_inp.wait()
    stat_s[...] = jnp.zeros_like(stat_s)
    for g in range(4):
        block_t = inp[2 * g : 2 * g + 2].reshape(128, 768).astype(F32).T
        lanes = pl.ds(g * 128, 128)
        stat_s[0:1, lanes] = jnp.sum(block_t, axis=0, keepdims=True)
        stat_s[1:2, lanes] = jnp.sum(block_t * block_t, axis=0, keepdims=True)
        n_t[:, lanes] = block_t.astype(BF16)
    c_stat = [push(stat_s, stat_r.at[d], x_dev[d]) for d in range(3)]

    c_att.wait_recv()

    @pl.loop(0, 3)
    def _(n):
        cols = span(n * 256, 256)
        acc = tn(att[0], cot[0, :, :, :, cols].reshape(512, 256))
        acc += tn(att[1], cot[1, :, :, :, cols].reshape(512, 256))
        wga[:, cols] = acc

    ysa[...] = wga[span((2 * y_other + core) * 96, 96), :].astype(BF16)
    c_a = push(ysa, yra, ylo_dev)

    c_pay.wait_recv()
    go[mine] = (pay_s[...] + pay_r[...]).astype(BF16)
    c_go = [push(go.at[mine], go.at[mine], dev) for dev in x_dev]
    c_phy = {(0, 0): hidden_sum(0, 0, c_ph[0, 0])}
    c_phy[0, 1] = hidden_sum(0, 1, c_ph[0, 1])

    for cp in c_stat:
        cp.wait_recv()
    stat_y[...] = stat_s[...] + stat_r[0] + stat_r[1] + stat_r[2]
    c_staty = push(stat_y, stat_r.at[3], yhi_dev)

    c_gp = {(0, 0): hidden_slope(0, 0, c_phy[0, 0])}
    c_phy[1, 0] = hidden_sum(1, 0, c_ph[1, 0])
    c_gp[0, 1] = hidden_slope(0, 1, c_phy[0, 1])
    c_phy[1, 1] = hidden_sum(1, 1, c_ph[1, 1])

    c_staty.wait_recv()
    stat = stat_y[...] + stat_r[3]
    mean_r = stat[0:1] / width
    inv_r = lax.rsqrt(stat[1:2] / width - mean_r * mean_r + EPS)

    @pl.loop(0, 8)
    def _(k):
        rows = span(k * 96, 96)
        n_t[rows, :] = ((n_t[rows, :].astype(F32) - mean_r) * inv_r).astype(BF16)

    c_nt = [
        push(n_t.at[span((2 * j + 1 - core) * 192, 192)], n_p.at[j, :, pl.ds(512, 512)], sib_dev)
        for j in range(2)
    ]
    l_nt = []
    for j in range(2):
        cp = pltpu.make_async_copy(
            n_t.at[span((2 * j + core) * 192, 192)], n_p.at[j, :, pl.ds(0, 512)], load_sem.at[8 + j]
        )
        cp.start()
        l_nt.append(cp)

    for cp in c_go:
        cp.wait_recv()
    attention_back(0)
    c_gp[1, 0] = hidden_slope(1, 0, c_phy[1, 0])
    gather_far(hidden_chunk(0, 0), c_gp[0, 0])
    c_gp[1, 1] = hidden_slope(1, 1, c_phy[1, 1])
    gather_far(hidden_chunk(0, 1), c_gp[0, 1])
    attention_back(1)
    c_gf = push(gf.at[0], gf.at[1], sib_dev)
    for cp in c_nt:
        cp.wait_recv()
    for cp in l_nt:
        cp.wait()
    gather_far(hidden_chunk(1, 0), c_gp[1, 0])
    c_gf.wait_recv()

    @pl.loop(0, 3)
    def _(n):
        acc = nn(n_p[...].reshape(384, 1024), gf[:, n].reshape(1024, 384))
        wgq[:, n] = acc.reshape(2, 192, 384)

    ysq[...] = wgq[y_other].astype(BF16)
    c_q = push(ysq, yrq, ylo_dev)

    gather_far(hidden_chunk(1, 1), c_gp[1, 1])
    c_gps = [share(0, 0), share(0, 1)]

    l_wqkv.wait()
    l_wup.wait()

    @pl.loop(0, 6)
    def _(i):
        b, n = i // 3, i % 3
        cols = span(n * 256, 256)
        rows = span(b * 256, 256)
        acc = nt(gf[0, 0, rows, :], wqkv[0, cols, :])
        acc += nt(gf[0, 1, rows, :], wqkv[1, cols, :])
        acc += nt(gf[0, 2, rows, :], wqkv[2, cols, :])
        tot[pl.ds(b * 4, 4), :, :, cols] = acc.reshape(4, 2, 32, 256)

    def grad_up(c):
        @pl.loop(0, 3)
        def _(n):
            cols = span(n * 256, 256)
            acc = nn(n_p[...].reshape(384, 1024), gp[:, c, :, :, :, cols].reshape(1024, 256))
            wgu[c, :, :, cols] = acc.reshape(2, 192, 256)

        ysu[c] = wgu[c, y_other].astype(BF16)
        return push(ysu.at[c], yru.at[c], ylo_dev)

    for cp in c_gps:
        cp.wait_recv()
    c_u = [grad_up(0)]

    c_z = []
    c_gps = []
    for p in range(2):
        c_gps.append(share(1, p))

        @pl.loop(0, 3)
        def _(n):
            cols = span(n * 256, 256)
            acc = nt(gp[0, 0, :, p].reshape(256, 768), wup[cols, 0:768])
            acc += nt(gp[0, 1, :, p].reshape(256, 768), wup[cols, 768:1536])
            acc = acc.reshape(8, 32, 256) + tot[:, p, :, cols]
            tot[:, p, :, cols] = acc
            zs[p, :, :, cols] = acc.astype(BF16)

        c_z.append([push(zs.at[p, z_of[d]], zr.at[p, d], z_dev[d]) for d in range(7)])

    for cp in c_gps:
        cp.wait_recv()
    c_u.append(grad_up(1))
    activate(y_lo)
    c_hid.append(push(hid.at[2 * y_lo + 1 - core], hid_s.at[y_lo], sib_dev))
    c_hid[1].wait_recv()
    down(y_lo)

    lane = lax.broadcasted_iota(jnp.int32, (64, 512), 1)
    token = lax.broadcasted_iota(jnp.int32, (64, 512), 0)
    pick = jnp.where(lane == token + col * 64, 1.0, 0.0).astype(F32)
    mean_c = jnp.sum(pick * mean_r, axis=1, keepdims=True)
    inv_c = jnp.sum(pick * inv_r, axis=1, keepdims=True)
    normed = (inp[col].reshape(64, 768).astype(F32) - mean_c) * inv_c
    gn = []
    for p in range(2):
        for cp in c_z[p]:
            cp.wait_recv()
        value = tot[col, p]
        for d in range(7):
            value = value + zr[p, d].astype(F32)
        gn.append(value)
    grad_n = jnp.concatenate(gn, axis=0)
    sum_g = jnp.sum(grad_n, axis=1, keepdims=True)
    sum_c = jnp.sum(grad_n * normed, axis=1, keepdims=True)
    lane = lax.broadcasted_iota(jnp.int32, (64, 128), 1)
    token = lax.broadcasted_iota(jnp.int32, (64, 128), 0)
    eye = jnp.where(lane == token, 1.0, 0.0).astype(F32)
    fin_s[...] = jnp.zeros_like(fin_s)
    fin_s[0:1, :] = jnp.sum(eye * sum_g, axis=0, keepdims=True)
    fin_s[1:2, :] = jnp.sum(eye * sum_c, axis=0, keepdims=True)
    c_fin = [push(fin_s, fin_r.at[d], x_dev[d]) for d in range(3)]

    c_d.wait_recv()
    gdown_o[...] = (wgd[y_lo] + yrd[...].astype(F32)).astype(BF16)
    c_a.wait_recv()
    gattn_o[...] = (
        wga[span((2 * y_lo + core) * 96, 96), :] + yra[...].astype(F32)
    ).astype(BF16)

    for cp in c_fin:
        cp.wait_recv()
    fin_y[...] = fin_s[...] + fin_r[0] + fin_r[1] + fin_r[2]
    c_finy = push(fin_y, fin_r.at[3], yhi_dev)

    c_q.wait_recv()
    gqkv_o[...] = (wgq[y_lo] + yrq[...].astype(F32)).astype(BF16)

    c_finy.wait_recv()
    fin = fin_y[...] + fin_r[3]
    mean_g = jnp.sum(eye * fin[0:1], axis=1, keepdims=True) / width
    mean_x = jnp.sum(eye * fin[1:2], axis=1, keepdims=True) / width
    branch = grad_n - mean_g - normed * mean_x
    result = cot[0, col].reshape(64, 768).astype(F32) + inv_c * branch
    gin_o[...] = result.astype(BF16)

    for c in range(2):
        c_u[c].wait_recv()
        gup_o[:, c * 768 : (c + 1) * 768] = (
            wgu[c, y_lo] + yru[c].astype(F32)
        ).astype(BF16)

    for cp in sent:
        cp.wait_send()
    assert len(sent) == N_COPIES, len(sent)


def hand_over(*refs):
    sem = refs[15]
    copies_in = [pltpu.make_async_copy(refs[i], refs[10 + i], sem.at[i]) for i in range(5)]
    copies_out = [pltpu.make_async_copy(refs[10 + i], refs[5 + i], sem.at[5 + i]) for i in range(5)]
    for cp in copies_in:
        cp.start()
    for first, second in zip(copies_in, copies_out):
        first.wait()
        second.start()
    for cp in copies_out:
        cp.wait()


def body(inputs, saved_qkv, saved_up, cotangent, weight_qkv, weight_up, weight_attn, weight_down):
    vm = pltpu.VMEM
    scratch = [
        vm((8, 2, 32, 768), BF16), vm((3, 512, 384), BF16), vm((8, 2, 32, 1536), BF16),
        vm((2, 8, 2, 32, 768), BF16),
        vm((3, 768, 384), BF16), vm((768, 1536), BF16), vm((384, 768), BF16), vm((1536, 768), BF16),
        vm((8, 512), F32), vm((4, 8, 512), F32), vm((8, 512), F32),
        vm((8, 2, 32, 384), F32), vm((3, 2, 2, 32, 384), F32),
        vm((2, 2, 32, 384), F32), vm((2, 2, 32, 384), F32),
        vm((2, 8, 2, 32, 768), F32), vm((2, 8, 2, 32, 768), BF16),
        vm((2, 2, 3, 2, 32, 768), BF16), vm((2, 2, 2, 32, 768), F32),
        vm((2, 2, 2, 32, 768), BF16), vm((2, 2, 2, 32, 768), BF16),
        vm((8, 2, 32, 384), BF16), vm((2, 2, 8, 2, 32, 768), BF16), vm((2, 3, 512, 384), BF16),
        vm((4, 8, 2, 32, 384), BF16), vm((2, 8, 2, 32, 384), BF16), vm((2, 512, 384), BF16),
        vm((768, 512), BF16), vm((2, 192, 1024), BF16),
        vm((6, 256, 256), F32), vm((512, 384), BF16), vm((512, 384), BF16),
        vm((8, 2, 32, 768), F32), vm((2, 8, 32, 768), BF16), vm((2, 7, 32, 768), BF16),
        vm((8, 128), F32), vm((4, 8, 128), F32), vm((8, 128), F32),
        vm((2, 384, 768), F32), vm((384, 768), F32), vm((2, 3, 192, 384), F32),
        vm((2, 2, 192, 768), F32),
        vm((384, 768), BF16), vm((384, 768), BF16), vm((96, 768), BF16), vm((96, 768), BF16),
        vm((3, 192, 384), BF16), vm((3, 192, 384), BF16),
        vm((2, 192, 768), BF16), vm((2, 192, 768), BF16),
        pltpu.SemaphoreType.DMA((10,)),
        pltpu.SemaphoreType.DMA((N_COPIES,)),
        pltpu.SemaphoreType.DMA((N_COPIES,)),
    ]
    results = pl.pallas_call(
        kernel,
        out_shape=(
            jax.ShapeDtypeStruct((64, 768), BF16),
            jax.ShapeDtypeStruct((3, 192, 384), BF16),
            jax.ShapeDtypeStruct((192, 1536), BF16),
            jax.ShapeDtypeStruct((96, 768), BF16),
            jax.ShapeDtypeStruct((384, 768), BF16),
        ),
        in_specs=[pl.BlockSpec(memory_space=pl.ANY)] * 8,
        out_specs=[pl.BlockSpec(memory_space=pltpu.VMEM)] * 5,
        scratch_shapes=scratch,
        compiler_params=pltpu.CompilerParams(
            collective_id=0, has_side_effects=True, vmem_limit_bytes=58 * 2**20
        ),
        name="layer_backward",
    )(
        inputs.reshape(8, 2, 32, 768),
        saved_qkv.transpose(1, 0, 2),
        saved_up.reshape(8, 2, 32, 1536),
        cotangent.reshape(8, 2, 32, 768),
        weight_qkv.transpose(1, 0, 2),
        weight_up,
        weight_attn,
        weight_down,
    )
    gin, gqkv, gup, gattn, gdown = pl.pallas_call(
        hand_over,
        out_shape=tuple(jax.ShapeDtypeStruct(r.shape, r.dtype) for r in results),
        in_specs=[pl.BlockSpec(memory_space=pl.ANY)] * 5,
        out_specs=[pl.BlockSpec(memory_space=pl.ANY)] * 5,
        scratch_shapes=[vm(r.shape, r.dtype) for r in results] + [pltpu.SemaphoreType.DMA((10,))],
        name="hand_over",
    )(*results)
    return (
        gin,
        gqkv.transpose(1, 0, 2).reshape(1, 1, 192, 3, 384),
        gup.reshape(1, 1, 192, 1536),
        gattn.reshape(1, 1, 96, 768),
        gdown.reshape(1, 1, 384, 768),
    )


def solution(mesh):
    return jax.shard_map(
        body,
        mesh=mesh,
        in_specs=(
            P("dp", "row"),
            P("dp", None, "col"),
            P("dp", "col"),
            P("dp", "row"),
            P("row", None, "col"),
            P("row", "col"),
            P("col", "row"),
            P("col", "row"),
        ),
        out_specs=(
            P(("dp", "col"), "row"),
            P("row", "dp", None, None, "col"),
            P("row", "dp", None, "col"),
            P("col", "dp", None, "row"),
            P("col", "dp", None, "row"),
        ),
        check_vma=False,
    )
```

time: 105 us -> 89.2 us (0.85)
  local copies, waits for them, and re-layouts: 12 us -> 0 us
  Pallas kernels: 91.9 us -> 87.3 us
    pallas_call x1, Pallas kernels: 91.9 us -> 84.9 us  [body(): pl.pallas_call(kernel, out_shape=(jax.ShapeDtypeStruct((64, 768), BF16),...]
    unnamed x17 -> x0, local copies, waits for them, and re-layouts: 6.76 us -> none
    reshape x3 -> x0, local copies, waits for them, and re-layouts: 5.21 us -> none  [the longest x1 2.25 us: body(): weight_qkv.reshape(768, 1152)]
    pallas_call x0 -> x1, Pallas kernels: none -> 2.4 us  [body(): pl.pallas_call(hand_over, out_shape=tuple((jax.ShapeDtypeStruct(r.shape,...]
where the time goes in v2:
time: 89.2 us; the launch traced here: 87.9 us
  Pallas kernels  87.3 us (98%)
    pallas_call x1, Pallas kernels, body(): pl.pallas_call(kernel, out_shape=(jax.ShapeDtypeStruct((64, 768), BF16),...  84.9 us
    pallas_call x1, Pallas kernels, body(): pl.pallas_call(hand_over, out_shape=tuple((jax.ShapeDtypeStruct(r.shape,...  2.4 us

profile of v2, /device:TPU:24, one launch (start us, length us, event | category | flops | bytes accessed | tf_op | source)
XLA Modules:
  0.0 87.9 jit_solution(12749390015201537660)
XLA Ops:
  0.6 84.9 %layer_backward.1 = (bf16[64,768]{1,0:T(8,128)(2,1)}, bf16[3,192,384]{2,1,0:T(8,128)(2,1)}, bf16[192,1536]{1,0:T(8,128)(2,1)}, bf16[96,768]{1,0:T(8,128)(2,1)}, bf16[384,768]{1,0:T(8,128)(2,1)}) custom-call(bf16[8,2,32,768]{3,2,1,0:T(8,128)(2,1)} %bitcast.14, bf16[3,512,384]{2,1,0:T(8,128)(2,1)} %bitcast.13, bf16[8,2,32,1536]{3,2,1,0:T(8,128)(2,1)} %bitcast.12, ...), custom_call_target="tpu_custom_call" | custom-call | tf_op jit(solution)/shard_map/layer_backward/pallas_call | solution.py:506
  85.5 2.4 %hand_over.1 = (bf16[64,768]{1,0:T(8,128)(2,1)}, bf16[3,192,384]{2,1,0:T(8,128)(2,1)}, bf16[192,1536]{1,0:T(8,128)(2,1)}, bf16[96,768]{1,0:T(8,128)(2,1)}, bf16[384,768]{1,0:T(8,128)(2,1)}) custom-call(bf16[64,768]{1,0:T(8,128)(2,1)} %get-tuple-element.15.refs_0_, bf16[3,192,384]{2,1,0:T(8,128)(2,1)} %get-tuple-element.16.refs_1_, ...), custom_call_target="tpu_custom_call" | custom-call | tf_op jit(solution)/shard_map/hand_over/pallas_call | solution.py:532

commit v3 on v2

--- a/solution.py
+++ b/solution.py
@@ -13,7 +13,7 @@
 INV_ROOT_TWO_PI = 0.3989422804014327
 F32 = jnp.float32
 BF16 = jnp.bfloat16
-N_COPIES = 85
+N_COPIES = 86
 
 
 def nt(a, b):
@@ -60,7 +60,7 @@
     inp, qkv, up, cot, wqkv, wup, wattn, wdown,
     stat_s, stat_r, stat_y,
     pa, pa_r, pay_s, pay_r,
-    ph, phb, ph_r, phx, phy_s, phy_r,
+    ph, phb, ph_r, phx, phw_r, phy_s, phy_r,
     go, gp, gf, hid, hid_s, att, n_t, n_p, probs_v, qn_v, kn_v,
     tot, zs, zr, fin_s, fin_r, fin_y,
     wgd, wga, wgq, wgu, ysd, yrd, ysa, yra, ysq, yrq, ysu, yru,
@@ -180,8 +180,10 @@
         for d in range(3):
             total = total + ph_r[c, p, d].astype(F32)
         phx[c, p] = total
-        phy_s[c, p] = total.astype(BF16)
-        return push(phy_s.at[c, p], phy_r.at[c, p], yhi_dev)
+        if c == 0:
+            return push(phx.at[c, p], phw_r.at[p], yhi_dev)
+        phy_s[p] = total.astype(BF16)
+        return push(phy_s.at[p], phy_r.at[p], yhi_dev)
 
     def hidden_chunk(c, p):
         return lambda r: gp.at[0, c, r, p]
@@ -190,7 +192,7 @@
         slope = gelu_slope(up[pl.ds(2 * x, 2), p, :, c * 768 : (c + 1) * 768].astype(F32))
         cp.wait_recv()
         gp[0, c, pl.ds(2 * x, 2), p] = (
-            (phx[c, p] + phy_r[c, p].astype(F32)) * slope
+            (phx[c, p] + (phw_r[p] if c == 0 else phy_r[p].astype(F32))) * slope
         ).astype(BF16)
         return gather(hidden_chunk(c, p))
 
@@ -248,7 +250,7 @@
     c_hid[0].wait_recv()
     down(y_other)
     ysd[...] = wgd[y_other].astype(BF16)
-    c_d = push(ysd, yrd, ylo_dev)
+    c_d = [push(ysd.at[0:192], yrd.at[0:192], ylo_dev)]
 
     c_ph[0, 1] = hidden_start(0, 1)
     c_ph[1, 0] = hidden_start(1, 0)
@@ -286,11 +288,14 @@
         wga[:, cols] = acc
 
     ysa[...] = wga[span((2 * y_other + core) * 96, 96), :].astype(BF16)
-    c_a = push(ysa, yra, ylo_dev)
-
+
+    activate(y_lo)
+    c_hid.append(push(hid.at[2 * y_lo + 1 - core], hid_s.at[y_lo], sib_dev))
     c_pay.wait_recv()
     go[mine] = (pay_s[...] + pay_r[...]).astype(BF16)
     c_go = [push(go.at[mine], go.at[mine], dev) for dev in x_dev]
+    c_hid[1].wait_recv()
+    down(y_lo)
     c_phy = {(0, 0): hidden_sum(0, 0, c_ph[0, 0])}
     c_phy[0, 1] = hidden_sum(0, 1, c_ph[0, 1])
 
@@ -303,6 +308,8 @@
     c_phy[1, 0] = hidden_sum(1, 0, c_ph[1, 0])
     c_gp[0, 1] = hidden_slope(0, 1, c_phy[0, 1])
     c_phy[1, 1] = hidden_sum(1, 1, c_ph[1, 1])
+    c_d.append(push(ysd.at[192:384], yrd.at[192:384], ylo_dev))
+    c_a = push(ysa, yra, ylo_dev)
 
     c_staty.wait_recv()
     stat = stat_y[...] + stat_r[3]
@@ -330,16 +337,16 @@
         cp.wait_recv()
     attention_back(0)
     c_gp[1, 0] = hidden_slope(1, 0, c_phy[1, 0])
-    gather_far(hidden_chunk(0, 0), c_gp[0, 0])
-    c_gp[1, 1] = hidden_slope(1, 1, c_phy[1, 1])
-    gather_far(hidden_chunk(0, 1), c_gp[0, 1])
     attention_back(1)
     c_gf = push(gf.at[0], gf.at[1], sib_dev)
+    c_gp[1, 1] = hidden_slope(1, 1, c_phy[1, 1])
+    gather_far(hidden_chunk(0, 0), c_gp[0, 0])
+    gather_far(hidden_chunk(0, 1), c_gp[0, 1])
     for cp in c_nt:
         cp.wait_recv()
     for cp in l_nt:
         cp.wait()
-    gather_far(hidden_chunk(1, 0), c_gp[1, 0])
+
     c_gf.wait_recv()
 
     @pl.loop(0, 3)
@@ -350,6 +357,7 @@
     ysq[...] = wgq[y_other].astype(BF16)
     c_q = push(ysq, yrq, ylo_dev)
 
+    gather_far(hidden_chunk(1, 0), c_gp[1, 0])
     gather_far(hidden_chunk(1, 1), c_gp[1, 1])
     c_gps = [share(0, 0), share(0, 1)]
 
@@ -399,11 +407,6 @@
     for cp in c_gps:
         cp.wait_recv()
     c_u.append(grad_up(1))
-    activate(y_lo)
-    c_hid.append(push(hid.at[2 * y_lo + 1 - core], hid_s.at[y_lo], sib_dev))
-    c_hid[1].wait_recv()
-    down(y_lo)
-
     lane = lax.broadcasted_iota(jnp.int32, (64, 512), 1)
     token = lax.broadcasted_iota(jnp.int32, (64, 512), 0)
     pick = jnp.where(lane == token + col * 64, 1.0, 0.0).astype(F32)
@@ -429,7 +432,8 @@
     fin_s[1:2, :] = jnp.sum(eye * sum_c, axis=0, keepdims=True)
     c_fin = [push(fin_s, fin_r.at[d], x_dev[d]) for d in range(3)]
 
-    c_d.wait_recv()
+    for cp in c_d:
+        cp.wait_recv()
     gdown_o[...] = (wgd[y_lo] + yrd[...].astype(F32)).astype(BF16)
     c_a.wait_recv()
     gattn_o[...] = (
@@ -487,7 +491,7 @@
         vm((2, 2, 32, 384), F32), vm((2, 2, 32, 384), F32),
         vm((2, 8, 2, 32, 768), F32), vm((2, 8, 2, 32, 768), BF16),
         vm((2, 2, 3, 2, 32, 768), BF16), vm((2, 2, 2, 32, 768), F32),
-        vm((2, 2, 2, 32, 768), BF16), vm((2, 2, 2, 32, 768), BF16),
+        vm((2, 2, 32, 768), F32), vm((2, 2, 32, 768), BF16), vm((2, 2, 32, 768), BF16),
         vm((8, 2, 32, 384), BF16), vm((2, 2, 8, 2, 32, 768), BF16), vm((2, 3, 512, 384), BF16),
         vm((4, 8, 2, 32, 384), BF16), vm((2, 8, 2, 32, 384), BF16), vm((2, 512, 384), BF16),
         vm((768, 512), BF16), vm((2, 192, 1024), BF16),

time: 89.2 us -> 89.3 us (level)
  no operation moved by 1% of the time
where the time goes in v3:
time: 89.3 us; the launch traced here: 87.6 us
  Pallas kernels  87 us (97%)
    pallas_call x1, Pallas kernels, body(): pl.pallas_call(kernel, out_shape=(jax.ShapeDtypeStruct((64, 768), BF16),...  84.6 us
    pallas_call x1, Pallas kernels, body(): pl.pallas_call(hand_over, out_shape=tuple((jax.ShapeDtypeStruct(r.shape,...  2.4 us

profile of v3, /device:TPU:24, one launch (start us, length us, event | category | flops | bytes accessed | tf_op | source)
XLA Modules:
  0.0 87.6 jit_solution(1900306979757892882)
XLA Ops:
  0.6 84.6 %layer_backward.1 = (bf16[64,768]{1,0:T(8,128)(2,1)}, bf16[3,192,384]{2,1,0:T(8,128)(2,1)}, bf16[192,1536]{1,0:T(8,128)(2,1)}, bf16[96,768]{1,0:T(8,128)(2,1)}, bf16[384,768]{1,0:T(8,128)(2,1)}) custom-call(bf16[8,2,32,768]{3,2,1,0:T(8,128)(2,1)} %bitcast.14, bf16[3,512,384]{2,1,0:T(8,128)(2,1)} %bitcast.13, bf16[8,2,32,1536]{3,2,1,0:T(8,128)(2,1)} %bitcast.12, ...), custom_call_target="tpu_custom_call" | custom-call | tf_op jit(solution)/shard_map/layer_backward/pallas_call | solution.py:510
  85.2 2.4 %hand_over.1 = (bf16[64,768]{1,0:T(8,128)(2,1)}, bf16[3,192,384]{2,1,0:T(8,128)(2,1)}, bf16[192,1536]{1,0:T(8,128)(2,1)}, bf16[96,768]{1,0:T(8,128)(2,1)}, bf16[384,768]{1,0:T(8,128)(2,1)}) custom-call(bf16[64,768]{1,0:T(8,128)(2,1)} %get-tuple-element.15.refs_0_, bf16[3,192,384]{2,1,0:T(8,128)(2,1)} %get-tuple-element.16.refs_1_, ...), custom_call_target="tpu_custom_call" | custom-call | tf_op jit(solution)/shard_map/hand_over/pallas_call | solution.py:536
